TPU v7x, 32 devices: a whole 2x2x4 slice. The times are simulated.
32 devices in a mesh: groups: 2 (over x), row: 16 (over z, y, core).
Axes of the slice: x: 2, y: 2, z: 4, core: 2. Of those that a mesh axis runs over, the one named last changes fastest.
Arguments:
- features: float32 [8, 16384], P(None, ('groups', 'row')), parts along dimension 1, may hold values from 0 to 1
- inv_length: float32 [16], P('groups'), parts along dimension 0, may hold values from 3 to 6
- outscale: float32 [2], P('groups'), parts along dimension 0, may hold values from 0.5 to 2
- noise_var: float32 [2], P('groups'), parts along dimension 0, may hold values from 0.01 to 0.1
- solution: float32 [16, 16384], P(None, ('groups', 'row')), parts along dimension 1, may hold values from -6 to 6
- residual: float32 [16, 16384], P(None, ('groups', 'row')), parts along dimension 1, may hold values from -10 to 10
- direction: float32 [16, 16384], P(None, ('groups', 'row')), parts along dimension 1, may hold values from -10 to 10
Outputs:
- new_solution: float32 [16, 16384], P(None, ('groups', 'row')), parts along dimension 1
- new_residual: float32 [16, 16384], P(None, ('groups', 'row')), parts along dimension 1
- new_direction: float32 [16, 16384], P(None, ('groups', 'row')), parts along dimension 1
There are 2 independent parts, one for each index of `groups`. A program takes and returns all parts, laid end to end along the dimension named above; each array names one. Nothing has to cross between parts.
All inputs are finite; a program needn't handle non-finite values.
Results may differ from a plain program's by a relative error of at most 0.00015.
Values sent between devices are 32-bit elements; how exact they have to be, the bound alone decides.
A program may use at most 64 MiB of HBM per device.

v0:
```python
import jax
import jax.numpy as jnp
from jax import lax
from jax.sharding import PartitionSpec as P


def kernel_block(zrow, zcolumn, out_scale):
    cross_term = lax.dot_general(
        zrow,
        zcolumn,
        (((0,), (0,)), ((), ())),
        precision=lax.Precision.HIGHEST,
        preferred_element_type=jnp.float32,
    )
    dist_sq = (
        jnp.sum(zrow * zrow, 0)[:, None] + jnp.sum(zcolumn * zcolumn, 0)[None, :] - 2.0 * cross_term
    )
    scaled_dist = jnp.sqrt(5.0 * jnp.maximum(dist_sq, 0.0))
    return out_scale * (1.0 + scaled_dist + scaled_dist * scaled_dist / 3.0) * jnp.exp(-scaled_dist)


def shards(features, inv_length, outscale, noise_var, solution, residual, direction):
    block_rows = features.shape[1]
    my_index = lax.axis_index("row")
    out_scale = outscale[0]
    scaled = features * inv_length[:, None]
    norm_old = lax.psum(jnp.sum(residual * residual, 1), "row")
    all_scaled, all_direction = (
        lax.all_gather(scaled, "row", axis=1, tiled=True),
        lax.all_gather(direction, "row", axis=1, tiled=True),
    )

    def block_of(source, which):
        return lax.dynamic_slice_in_dim(source, which * block_rows, block_rows, 1)

    def row_product(which, own_terms):
        kernel_tile = kernel_block(scaled, block_of(all_scaled, which), out_scale)
        far_direction = block_of(all_direction, which)
        own_terms = own_terms + lax.dot_general(
            far_direction,
            kernel_tile,
            (((1,), (1,)), ((), ())),
            precision=lax.Precision.HIGHEST,
            preferred_element_type=jnp.float32,
        )
        return (kernel_tile, own_terms)

    def both_products(which, loop_state):
        own_terms, mirrored = loop_state
        kernel_tile, own_terms = row_product(which, own_terms)
        column_terms = jnp.dot(
            direction,
            kernel_tile,
            precision=lax.Precision.HIGHEST,
            preferred_element_type=jnp.float32,
        )
        weight_off = (which != my_index).astype(jnp.float32)
        updated = block_of(mirrored, which) + weight_off * column_terms
        mirrored = lax.dynamic_update_slice_in_dim(mirrored, updated, which * block_rows, 1)
        return (own_terms, mirrored)

    zero_own = jnp.zeros(direction.shape, jnp.float32)
    zero_whole = jnp.zeros(all_direction.shape, jnp.float32)
    own_terms, mirrored = lax.fori_loop(0, my_index + 1, both_products, (zero_own, zero_whole))
    kernel_sum = own_terms + lax.psum_scatter(mirrored, "row", scatter_dimension=1, tiled=True)
    image_sum = kernel_sum + noise_var[0] * direction
    curvature = lax.psum(jnp.sum(direction * image_sum, 1), "row")
    step_size = norm_old / curvature
    new_residual = residual - step_size[:, None] * image_sum
    norm_new = lax.psum(jnp.sum(new_residual * new_residual, 1), "row")
    new_solution = solution + step_size[:, None] * direction
    new_direction = new_residual + (norm_new / norm_old)[:, None] * direction
    return (new_solution, new_residual, new_direction)


def solution(mesh):
    return jax.shard_map(
        shards,
        mesh=mesh,
        in_specs=(
            P(None, ("groups", "row")),
            P("groups"),
            P("groups"),
            P("groups"),
            P(None, ("groups", "row")),
            P(None, ("groups", "row")),
            P(None, ("groups", "row")),
        ),
        out_specs=(
            P(None, ("groups", "row")),
            P(None, ("groups", "row")),
            P(None, ("groups", "row")),
        ),
        check_vma=False,
    )
```

profile of v0, /device:TPU:0, one launch (start us, length us, event | category | flops | bytes accessed | tf_op | source)
XLA Modules:
  0.0 238.7 jit_solution(9577700948602693813)
XLA Ops:
  7.2 0.0 copy-start.6
  7.2 0.0 reduce-scatter.2.cloned.1.call-start
  7.2 0.6 copy-done.6
  7.8 0.8 multiply_reduce_fusion.4
  8.6 0.0 copy-start.1
  8.6 23.8 %all_gather.7 = f32[8,8192]{1,0:T(8,128)S(1)} all-gather(f32[8,512]{1,0:T(8,128)S(1)} %get-tuple-element.235), channel_id=1, replica_groups=mesh['groups'=2,'row'=16] {'row'}, dimensions={1}, use_global_device_ids=true | all-gather | bytes 278528 | tf_op jit(solution)/shard_map/all_gather | solution.py:29
  32.4 0.0 copy-done.1
  32.4 18.9 %all_gather.6 = f32[16,8192]{1,0:T(8,128)S(1)} all-gather(f32[16,512]{1,0:T(8,128)S(1)} %copy-done.1), channel_id=1, replica_groups=mesh['groups'=2,'row'=16] {'row'}, dimensions={1}, use_global_device_ids=true | all-gather | bytes 557056 | tf_op jit(solution)/shard_map/all_gather | solution.py:30
  51.3 4.0 %while.14 = (s32[]{:T(128)}, f32[16,512]{1,0:T(8,128)S(1)}, f32[16,8192]{1,0:T(8,128)S(1)}, s32[]{:T(128)}, f32[16,8192]{1,0:T(8,128)S(1)}, /*index=5*/f32[]{:T(...) while((s32[]{:T(128)}, f32[16,512]{1,0:T(8,128)S(1)}, ...), condition=%wide.region_5.0_spmd, body=%wide.region_3.5_spmd.sunk | while | flops 129007104 | bytes 3397857 | solution.py:64
  51.4 2.3 exponential_multiply_fusion.2
  53.7 1.0 fusion.29
  54.7 0.6 convolution_add_fusion.2
  55.4 0.0 copy-start
  55.4 0.0 copy-start.4
  55.4 0.8 copy-done
  56.1 0.0 reduce-scatter.2.cloned.1.call-update
  56.8 0.0 copy-done.4
  56.8 0.1 multiply_reduce_fusion.3
  56.9 113.3 %reduce-scatter.2.cloned.1.call-done = f32[16,512]{1,0:T(8,128)} async-done(((f32[16,8192]{1,0:T(8,128)}), f32[16,512]{1,0:T(8,128)}) %reduce-scatter.2.cloned.1.call-update) | async-done | bytes 32784 | tf_op jit(solution)/shard_map/reduce_scatter | solution.py:65
  170.3 0.0 copy-start.2
  170.3 0.0 copy-start.5
  170.3 0.9 multiply_reduce_fusion.2
  171.2 29.6 %all-reduce = (f32[16]{0:T(128)S(1)}, f32[16]{0:T(128)S(1)}) all-reduce(f32[16]{0:T(128)S(1)} %multiply_reduce_fusion.3, f32[16]{0:T(128)S(1)} %multiply_reduce_fusion.2), channel_id=1, replica_groups=mesh['groups'=2,'row'=16] {'row'}, use_global_device_ids=true, to_apply=%region_1.0 | all-reduce | flops 32 | bytes 256 | tf_op jit(solution)/shard_map/psum | solution.py:27
  200.8 0.0 copy-done.2
  200.8 0.0 copy-done.5
  200.8 0.8 multiply_reduce_fusion.1
  201.6 0.0 copy-start.3
  201.7 29.5 %psum.23 = f32[16]{0:T(128)S(1)} all-reduce(f32[16]{0:T(128)S(1)} %get-tuple-element.154), channel_id=1, replica_groups=mesh['groups'=2,'row'=16] {'row'}, use_global_device_ids=true, to_apply=%region_10.0 | all-reduce | flops 16 | bytes 128 | tf_op jit(solution)/shard_map/psum | solution.py:70
  231.2 0.7 multiply_add_fusion
  231.8 0.0 copy-done.3
  (5 shorter events, 0.1 us)
Async XLA Ops:
  7.2 0.7 copy-start.6
  7.2 163.1 %reduce-scatter.2.cloned.1.call-start = ((), (), s32[]{:S(2)}) async-start(), calls=%async_computation.1 | async-start | bytes 557056 | tf_op jit(solution)/shard_map/reduce_scatter | solution.py:65
  8.6 23.8 %copy-start.1 = (f32[16,512]{1,0:T(8,128)S(1)}, f32[16,512]{1,0:T(8,128)}, u32[]{:S(2)}) copy-start(f32[16,512]{1,0:T(8,128)} %param.15) | copy-start | bytes 98308
  55.4 0.8 copy-start
  55.4 1.5 copy-start.4
  170.3 30.6 %copy-start.2 = (f32[16,512]{1,0:T(8,128)S(1)}, f32[16,512]{1,0:T(8,128)}, u32[]{:S(2)}) copy-start(f32[16,512]{1,0:T(8,128)} %reduce-scatter.2.cloned.1.call-done) | copy-start | bytes 98308
  170.3 30.6 %copy-start.5 = (f32[16,512]{1,0:T(8,128)S(1)}, f32[16,512]{1,0:T(8,128)}, u32[]{:S(2)}) copy-start(f32[16,512]{1,0:T(8,128)} %param.13) | copy-start | bytes 98308
  201.6 30.2 %copy-start.3 = (f32[16,512]{1,0:T(8,128)}, f32[16,512]{1,0:T(8,128)S(1)}, u32[]{:S(2)}) copy-start(f32[16,512]{1,0:T(8,128)S(1)} %get-tuple-element.155) | copy-start | bytes 98308
Sparse Core Ops, SparseCore 0:
  56.3 113.9 reduce-scatter.1
where the time goes:
time: 239 us
  waiting for transfers between devices  113 us (47%)
  blocking collectives  102 us (43%)
  between operations  14.7 us (6%)
  matrix products  3.94 us (2%)
  other arithmetic  3.4 us (1%)
    reduce_scatter x1, waiting for transfers between devices, shards(): lax.psum_scatter(mirrored, 'row', scatter_dimension=1, tiled=True)  113 us
    psum x1, blocking collectives, shards(): norm_old = lax.psum(jnp.sum(residual * residual, 1), 'row')  29.6 us
    psum x1, blocking collectives, shards(): norm_new = lax.psum(jnp.sum(new_residual * new_residual, 1), 'row')  29.5 us
    all_gather x1, blocking collectives, shards(): lax.all_gather(scaled, 'row', axis=1, tiled=True)  23.8 us
    all_gather x1, blocking collectives, shards(): lax.all_gather(direction, 'row', axis=1, tiled=True)  18.9 us
  transfers between devices with their start and end apart: 1, of which 1 were waited for; matrix products, arithmetic and copies ran while one was open for 0% of the time, Pallas kernels for 0%

commit v1 on v0

v1 whole, which is shorter than its diff:
```python
import functools
import math

import jax
import jax.numpy as jnp
from jax import lax
from jax.experimental import pallas as pl
from jax.experimental.pallas import tpu as pltpu
from jax.sharding import PartitionSpec as P

LN2 = math.log(2.0)
FOLD = math.sqrt(5.0) / LN2
QUAD = LN2 * LN2 / 3.0
LIN = 3.0 / LN2
CONST = 3.0 / (LN2 * LN2)
TINY = 1e-30
CHUNK = 256


def rounded(x):
    return x.astype(jnp.bfloat16).astype(jnp.float32)


def pieces(x):
    first = rounded(x)
    rest = x - first
    second = rounded(rest)
    return first, second, rounded(rest - second)


def norm_rows(z, norm_first):
    n1, n2, n3 = pieces(jnp.sum(z * z, 0, keepdims=True))
    row = lax.broadcasted_iota(jnp.int32, z.shape, 0)
    at = 0 if norm_first else 3
    out = jnp.where((row < 3) if not norm_first else ((row >= 3) & (row < 6)), 1.0, 0.0)
    out = jnp.where(row == at, n1, out)
    out = jnp.where(row == at + 1, n2, out)
    return jnp.where(row == at + 2, n3, out)


def far_factor(z):
    z1, z2, z3 = pieces(z)
    return jnp.concatenate(
        [z1, z1, z2, z1, z3, z2, norm_rows(z, True), jnp.zeros_like(z)], 0
    ).astype(jnp.bfloat16)


def near_factor(z):
    z1, z2, z3 = (-2.0 * piece for piece in pieces(z))
    return jnp.concatenate(
        [z1, z2, z1, z3, z1, z2, norm_rows(z, False), jnp.zeros_like(z)], 0
    ).astype(jnp.bfloat16)


def step_kernel(
    n,
    depth,
    features,
    inv_length,
    outscale,
    noise_var,
    solution,
    residual,
    direction,
    new_solution,
    new_residual,
    new_direction,
    held,
    near,
    total,
    mine,
    sums,
    send_sem,
    recv_sem,
    sum_send,
    sum_recv,
):
    feats = features.shape[0]
    points = features.shape[1]
    columns = direction.shape[0]
    chips = n // 2
    half = chips // 2
    me = lax.axis_index("row")
    core = me % 2
    chip = me // 2
    y = chip % depth
    z = chip // depth
    span = chips // depth
    pos = y * span + z + (y % 2) * (span - 1 - 2 * z)

    def device_at(ring):
        ring = ring % chips
        yy = ring // span
        zz = ring % span
        zz = zz + (yy % 2) * (span - 1 - 2 * zz)
        return (zz * depth + yy) * 2 + core

    right = device_at(pos + 1)
    left = device_at(pos + chips - 1)
    sibling = me + 1 - 2 * core

    barrier = pltpu.get_barrier_semaphore()

    def greet(k, carry):
        pl.semaphore_signal(
            barrier, inc=1, device_id={"row": (me + k) % n}, device_id_type=pl.DeviceIdType.MESH
        )
        return carry

    lax.fori_loop(1, n, greet, 0)

    row = lax.broadcasted_iota(jnp.int32, (feats, points), 0)
    scale = jnp.zeros((feats, points), jnp.float32)
    for f in range(feats):
        scale = jnp.where(row == f, inv_length[f] * FOLD, scale)
    scaled = (features[...] - 0.5) * scale
    held[0, 0:feats, :] = scaled
    held[0, feats:, :] = direction[...]
    near[...] = near_factor(scaled)
    total[...] = jnp.zeros_like(total)

    pl.semaphore_wait(barrier, n - 1)

    def copy(source, slot, device):
        return pltpu.make_async_remote_copy(
            src_ref=held.at[source],
            dst_ref=held.at[slot],
            send_sem=send_sem.at[slot],
            recv_sem=recv_sem.at[slot],
            device_id={"row": device},
            device_id_type=pl.DeviceIdType.MESH,
        )

    def work(slot):
        block = held[slot]
        far = far_factor(block[0:feats])
        d = block[feats:]
        d_high = rounded(d)
        both = jnp.concatenate([d_high, d - d_high], 0).astype(jnp.bfloat16)
        out = None
        for at in range(0, points, CHUNK):
            dist = lax.dot_general(
                far[:, at : at + CHUNK],
                near[...],
                (((0,), (0,)), ((), ())),
                preferred_element_type=jnp.float32,
            )
            dist = jnp.maximum(dist, TINY)
            b = dist * lax.rsqrt(dist)
            tile = ((b + LIN) * b + CONST) * jnp.exp2(-b)
            high = tile.astype(jnp.bfloat16)
            low = (tile - high.astype(jnp.float32)).astype(jnp.bfloat16)
            lhs = both[:, at : at + CHUNK]
            part = jnp.dot(lhs, high, preferred_element_type=jnp.float32) + jnp.dot(
                lhs, low, preferred_element_type=jnp.float32
            )
            out = part if out is None else out + part
        total[...] += out

    copy(0, 2, right).start()
    copy(0, 4, left).start()
    copy(0, 1, sibling).start()

    def own_pair(k, carry):
        @pl.when(k == 1)
        def _():
            copy(0, 1, sibling).wait_recv()

        work(k)
        return carry

    lax.fori_loop(0, 2, own_pair, 0)

    def ring_step(s, carry):
        first = 2 + 4 * s
        second = first + 2
        copy(0, first, right).wait_recv()
        copy(0, second, left).wait_recv()

        @pl.when(s < half - 2)
        def _():
            copy(first, first + 4, right).start()
            copy(second, second + 4, left).start()

        @pl.when(s == half - 2)
        def _():
            copy(first + 2 * core, first + 4, right + core * (left - right)).start()

        copy(first, first + 1, sibling).start()
        copy(second, second + 1, sibling).start()

        def one(k, inner):
            slot = first + 2 * (k % 2) + k // 2

            @pl.when(k >= 2)
            def _():
                copy(0, slot, sibling).wait_recv()

            work(slot)
            return inner

        return lax.fori_loop(0, 4, one, carry)

    lax.fori_loop(0, half - 1, ring_step, 0)

    copy(0, n - 2, right).wait_recv()
    copy(n - 2, n - 1, sibling).start()

    def last_pair(k, carry):
        @pl.when(k == 1)
        def _():
            copy(0, n - 1, sibling).wait_recv()

        work(n - 2 + k)
        return carry

    lax.fori_loop(0, 2, last_pair, 0)

    d = direction[...]
    r = residual[...]
    image = (total[0:columns] + total[columns:]) * (outscale[0] * QUAD) + noise_var[0] * d
    lane = lax.broadcasted_iota(jnp.int32, (columns, 128), 1)
    sub = lax.broadcasted_iota(jnp.int32, (columns, 128), 0)
    spread = jnp.zeros((columns, 128), jnp.float32)
    for k, product in enumerate((r * r, d * image, r * image, image * image)):
        spread = jnp.where(lane == sub + k * columns, jnp.sum(product, 1, keepdims=True), spread)
    mine[...] = jnp.sum(spread, 0, keepdims=True)

    def sum_copy(k):
        return pltpu.make_async_remote_copy(
            src_ref=mine,
            dst_ref=sums.at[k],
            send_sem=sum_send.at[k],
            recv_sem=sum_recv.at[k],
            device_id={"row": (me + k) % n},
            device_id_type=pl.DeviceIdType.MESH,
        )

    def send_sum(k, carry):
        sum_copy(k).start()
        return carry

    lax.fori_loop(1, n, send_sum, 0)
    sums[0] = mine[...]

    def drain(k, carry):
        copy(0, k, sibling).wait_send()
        return carry

    lax.fori_loop(1, n, drain, 0)

    def take_sum(k, carry):
        sum_copy(k).wait()
        return carry

    lax.fori_loop(1, n, take_sum, 0)
    whole = jnp.broadcast_to(jnp.sum(sums[...], 0), (columns, 128))
    rr, curv, ri, ii = (
        jnp.sum(jnp.where(lane == sub + k * columns, whole, 0.0), 1, keepdims=True)
        for k in range(4)
    )
    alpha = rr / curv
    rr_new = jnp.maximum(rr - 2.0 * alpha * ri + alpha * alpha * ii, 0.0)
    fresh = r - alpha * image
    new_solution[...] = solution[...] + alpha * d
    new_residual[...] = fresh
    new_direction[...] = fresh + (rr_new / rr) * d


def shards(n, depth, features, inv_length, outscale, noise_var, solution, residual, direction):
    feats, points = features.shape
    columns = direction.shape[0]
    vmem = pl.BlockSpec(memory_space=pltpu.VMEM)
    smem = pl.BlockSpec(memory_space=pltpu.SMEM)
    out = jax.ShapeDtypeStruct(direction.shape, jnp.float32)
    return pl.pallas_call(
        functools.partial(step_kernel, n, depth),
        out_shape=(out, out, out),
        in_specs=[vmem, smem, smem, smem, vmem, vmem, vmem],
        out_specs=(vmem, vmem, vmem),
        scratch_shapes=[
            pltpu.VMEM((n, feats + columns, points), jnp.float32),
            pltpu.VMEM((8 * feats, points), jnp.bfloat16),
            pltpu.VMEM((2 * columns, points), jnp.float32),
            pltpu.VMEM((1, 128), jnp.float32),
            pltpu.VMEM((n, 1, 128), jnp.float32),
            pltpu.SemaphoreType.DMA((n,)),
            pltpu.SemaphoreType.DMA((n,)),
            pltpu.SemaphoreType.DMA((n,)),
            pltpu.SemaphoreType.DMA((n,)),
        ],
        compiler_params=pltpu.CompilerParams(
            collective_id=0, has_side_effects=True, vmem_limit_bytes=24 * 1024 * 1024
        ),
    )(features, inv_length, outscale, noise_var, solution, residual, direction)


def solution(mesh):
    n = mesh.shape["row"]
    depth = 1
    while 4 * depth * depth <= n // 2:
        depth *= 2
    whole = P(None, ("groups", "row"))
    part = P("groups")
    return jax.shard_map(
        functools.partial(shards, n, depth),
        mesh=mesh,
        in_specs=(whole, part, part, part, whole, whole, whole),
        out_specs=(whole, whole, whole),
        check_vma=False,
    )
```

time: 239 us -> 34.8 us (0.15)
  waiting for transfers between devices: 113 us -> 0 us
  blocking collectives: 102 us -> 0 us
  Pallas kernels: 0 us -> 27.6 us
  between operations: 14.7 us -> 1.97 us
  matrix products: 3.94 us -> 0 us
  local copies, waits for them, and re-layouts: 1.43 us -> 4.83 us
  other arithmetic: 3.4 us -> 0 us
    reduce_scatter x1 -> x0, waiting for transfers between devices: 113 us -> none  [shards(): lax.psum_scatter(mirrored, 'row', scatter_dimension=1, tiled=True)]
    psum x2 -> x0, blocking collectives: 59.1 us -> none  [the longest x1 29.6 us: shards(): norm_old = lax.psum(jnp.sum(residual * residual, 1), 'row')]
    all_gather x2 -> x0, blocking collectives: 42.7 us -> none  [the longest x1 23.8 us: shards(): lax.all_gather(scaled, 'row', axis=1, tiled=True)]
    pallas_call x0 -> x1, Pallas kernels: none -> 27.6 us  [shards(): pl.pallas_call(functools.partial(step_kernel, n, depth), out_shape=(out,...]
    dot_general x3 -> x0, matrix products: 3.94 us -> none  [the longest x1 2.31 us: kernel_block(): lax.dot_general(zrow, zcolumn, (((0,), (0,)), ((), ())), precision=lax.Pr...]
    unnamed x14 -> x13, local copies, waits for them, and re-layouts: 1.39 us -> 4.83 us
    reduce_sum x5 -> x0, other arithmetic: 2.69 us -> none  [the longest x1 0.94 us: shards(): curvature = lax.psum(jnp.sum(direction * image_sum, 1), 'row')]
  transfers between devices with their start and end apart: 1 -> 0, of which waited for: 1 -> 0; matrix products, arithmetic and copies ran while one was open for 0% -> 0% of each run, Pallas kernels for 0% -> 0%
where the time goes in v1:
time: 34.8 us; the launch traced here: 34.4 us
  Pallas kernels  27.6 us (79%)
  local copies, waits for them, and re-layouts  4.83 us (14%)
  between operations  1.97 us (6%)
    pallas_call x1, Pallas kernels, shards(): pl.pallas_call(functools.partial(step_kernel, n, depth), out_shape=(out,...  27.6 us
    unnamed x13, local copies, waits for them, and re-layouts  4.83 us

profile of v1, /device:TPU:0, one launch (start us, length us, event | category | flops | bytes accessed | tf_op | source)
XLA Modules:
  0.0 34.4 jit_solution(2901939182054937257)
XLA Ops:
  1.3 0.0 copy-start.4
  1.9 0.0 copy-done.4
  2.0 0.0 copy-start
  2.0 0.7 %copy-done = f32[16,512]{1,0:T(8,128)S(1)} copy-done((f32[16,512]{1,0:T(8,128)S(1)}, f32[16,512]{1,0:T(8,128)}, u32[]{:S(2)}) %copy-start) | copy-done | bytes 32792
  2.7 0.0 copy-start.1
  2.7 0.8 %copy-done.1 = f32[16,512]{1,0:T(8,128)S(1)} copy-done((f32[16,512]{1,0:T(8,128)S(1)}, f32[16,512]{1,0:T(8,128)}, u32[]{:S(2)}) %copy-start.1) | copy-done | bytes 32792
  3.5 0.0 copy-start.2
  3.5 0.8 %copy-done.2 = f32[16,512]{1,0:T(8,128)S(1)} copy-done((f32[16,512]{1,0:T(8,128)S(1)}, f32[16,512]{1,0:T(8,128)}, u32[]{:S(2)}) %copy-start.2) | copy-done | bytes 32792
  4.2 0.0 copy-start.3
  4.2 0.7 %copy-done.3 = f32[8,512]{1,0:T(8,128)S(1)} copy-done((f32[8,512]{1,0:T(8,128)S(1)}, f32[8,512]{1,0:T(8,128)}, u32[]{:S(2)}) %copy-start.3) | copy-done | bytes 16408
  5.0 27.6 %shard_map.94 = (f32[16,512]{1,0:T(8,128)S(1)}, f32[16,512]{1,0:T(8,128)S(1)}, f32[16,512]{1,0:T(8,128)S(1)}) custom-call(f32[8,512]{1,0:T(8,128)S(1)} %copy-done.3, f32[8]{0:T(128)S(1)} %copy-done.4, f32[1]{0:T(128)S(6)} %copy.13.outscale, f32[1]{0:T(128)S(6)} %copy.14.noise_var, f32[16,512]{1,0:T(8,128)S(1)} %copy-done, f32[16,512]{1,0:T(8,128)S(1)} %copy-done.1, ...), custom_call_target="tpu_custom_call" | custom-call | tf_op jit(solution)/shard_map/pallas_call | solution.py:276
  32.6 0.6 %copy.15 = f32[16,512]{1,0:T(8,128)} copy(f32[16,512]{1,0:T(8,128)S(1)} %get-tuple-element.6) | data formatting | bytes 65536
  33.2 0.6 %copy.16 = f32[16,512]{1,0:T(8,128)} copy(f32[16,512]{1,0:T(8,128)S(1)} %get-tuple-element.7) | data formatting | bytes 65536
  33.8 0.6 %copy.17 = f32[16,512]{1,0:T(8,128)} copy(f32[16,512]{1,0:T(8,128)S(1)} %get-tuple-element.8) | data formatting | bytes 65536
Async XLA Ops:
  1.3 0.7 %copy-start.4 = (f32[8]{0:T(128)S(1)}, f32[8]{0:T(128)}, u32[]{:S(2)}) copy-start(f32[8]{0:T(128)} %inv_length.1) | copy-start | bytes 100
  2.0 0.8 %copy-start = (f32[16,512]{1,0:T(8,128)S(1)}, f32[16,512]{1,0:T(8,128)}, u32[]{:S(2)}) copy-start(f32[16,512]{1,0:T(8,128)} %solution.1) | copy-start | bytes 98308
  2.7 0.8 %copy-start.1 = (f32[16,512]{1,0:T(8,128)S(1)}, f32[16,512]{1,0:T(8,128)}, u32[]{:S(2)}) copy-start(f32[16,512]{1,0:T(8,128)} %residual.1) | copy-start | bytes 98308
  3.5 0.8 %copy-start.2 = (f32[16,512]{1,0:T(8,128)S(1)}, f32[16,512]{1,0:T(8,128)}, u32[]{:S(2)}) copy-start(f32[16,512]{1,0:T(8,128)} %direction.1) | copy-start | bytes 98308
  4.2 0.7 %copy-start.3 = (f32[8,512]{1,0:T(8,128)S(1)}, f32[8,512]{1,0:T(8,128)}, u32[]{:S(2)}) copy-start(f32[8,512]{1,0:T(8,128)} %features.1) | copy-start | bytes 49156

commit v2 on v1

--- a/solution.py
+++ b/solution.py
@@ -14,7 +14,6 @@
 LIN = 3.0 / LN2
 CONST = 3.0 / (LN2 * LN2)
 TINY = 1e-30
-CHUNK = 256
 
 
 def rounded(x):
@@ -55,16 +54,19 @@
 def step_kernel(
     n,
     depth,
+    features_hbm,
+    inv_length_hbm,
+    outscale_hbm,
+    noise_var_hbm,
+    residual_hbm,
+    direction_hbm,
+    image_out,
+    rates_out,
     features,
     inv_length,
     outscale,
     noise_var,
-    solution,
     residual,
-    direction,
-    new_solution,
-    new_residual,
-    new_direction,
     held,
     near,
     total,
@@ -74,10 +76,26 @@
     recv_sem,
     sum_send,
     sum_recv,
+    load_sem,
 ):
-    feats = features.shape[0]
-    points = features.shape[1]
-    columns = direction.shape[0]
+    feats, points = features.shape
+    columns = residual.shape[0]
+    direction = held.at[0, feats:]
+    loads = [
+        pltpu.make_async_copy(source, target, load_sem.at[k])
+        for k, (source, target) in enumerate(
+            (
+                (features_hbm, features),
+                (inv_length_hbm, inv_length),
+                (direction_hbm, direction),
+                (outscale_hbm, outscale),
+                (noise_var_hbm, noise_var),
+                (residual_hbm, residual),
+            )
+        )
+    ]
+    for load in loads:
+        load.start()
     chips = n // 2
     half = chips // 2
     me = lax.axis_index("row")
@@ -108,6 +126,8 @@
         return carry
 
     lax.fori_loop(1, n, greet, 0)
+    for load in loads[:3]:
+        load.wait()
 
     row = lax.broadcasted_iota(jnp.int32, (feats, points), 0)
     scale = jnp.zeros((feats, points), jnp.float32)
@@ -115,7 +135,6 @@
         scale = jnp.where(row == f, inv_length[f] * FOLD, scale)
     scaled = (features[...] - 0.5) * scale
     held[0, 0:feats, :] = scaled
-    held[0, feats:, :] = direction[...]
     near[...] = near_factor(scaled)
     total[...] = jnp.zeros_like(total)
 
@@ -131,34 +150,26 @@
             device_id_type=pl.DeviceIdType.MESH,
         )
 
-    def work(slot):
-        block = held[slot]
+    def work(slot, count):
+        block = jnp.concatenate([held[slot + k] for k in range(count)], 1)
         far = far_factor(block[0:feats])
         d = block[feats:]
         d_high = rounded(d)
         both = jnp.concatenate([d_high, d - d_high], 0).astype(jnp.bfloat16)
-        out = None
-        for at in range(0, points, CHUNK):
-            dist = lax.dot_general(
-                far[:, at : at + CHUNK],
-                near[...],
-                (((0,), (0,)), ((), ())),
-                preferred_element_type=jnp.float32,
-            )
-            dist = jnp.maximum(dist, TINY)
-            b = dist * lax.rsqrt(dist)
-            tile = ((b + LIN) * b + CONST) * jnp.exp2(-b)
-            high = tile.astype(jnp.bfloat16)
-            low = (tile - high.astype(jnp.float32)).astype(jnp.bfloat16)
-            lhs = both[:, at : at + CHUNK]
-            part = jnp.dot(lhs, high, preferred_element_type=jnp.float32) + jnp.dot(
-                lhs, low, preferred_element_type=jnp.float32
-            )
-            out = part if out is None else out + part
-        total[...] += out
+        dist = lax.dot_general(
+            far, near[...], (((0,), (0,)), ((), ())), preferred_element_type=jnp.float32
+        )
+        dist = jnp.maximum(dist, TINY)
+        b = dist * lax.rsqrt(dist)
+        tile = ((b + LIN) * b + CONST) * jnp.exp2(-b)
+        high = tile.astype(jnp.bfloat16)
+        low = (tile - high.astype(jnp.float32)).astype(jnp.bfloat16)
+        total[...] += jnp.dot(both, high, preferred_element_type=jnp.float32) + jnp.dot(
+            both, low, preferred_element_type=jnp.float32
+        )
 
     copy(0, 2, right).start()
-    copy(0, 4, left).start()
+    copy(0, 3, left).start()
     copy(0, 1, sibling).start()
 
     def own_pair(k, carry):
@@ -166,56 +177,52 @@
         def _():
             copy(0, 1, sibling).wait_recv()
 
-        work(k)
+        work(k, 1)
         return carry
 
     lax.fori_loop(0, 2, own_pair, 0)
 
-    def ring_step(s, carry):
-        first = 2 + 4 * s
-        second = first + 2
-        copy(0, first, right).wait_recv()
-        copy(0, second, left).wait_recv()
-
-        @pl.when(s < half - 2)
+    last = half * 2 - 2
+
+    def pair(p, carry):
+        first = 2 + 2 * p
+        second = first + 1
+
+        @pl.when((p % 2 == 0) & (p < last))
         def _():
-            copy(first, first + 4, right).start()
-            copy(second, second + 4, left).start()
-
-        @pl.when(s == half - 2)
+            copy(0, first, right).wait_recv()
+            copy(0, second, left).wait_recv()
+
+            @pl.when(p < last - 2)
+            def _():
+                copy(first, first + 4, right).start()
+                copy(second, second + 4, left).start()
+
+            @pl.when(p == last - 2)
+            def _():
+                copy(first + core, first + 4, right + core * (left - right)).start()
+
+            copy(first, first + 2, sibling).start()
+            copy(second, second + 2, sibling).start()
+
+        @pl.when(p % 2 == 1)
         def _():
-            copy(first + 2 * core, first + 4, right + core * (left - right)).start()
-
-        copy(first, first + 1, sibling).start()
-        copy(second, second + 1, sibling).start()
-
-        def one(k, inner):
-            slot = first + 2 * (k % 2) + k // 2
-
-            @pl.when(k >= 2)
-            def _():
-                copy(0, slot, sibling).wait_recv()
-
-            work(slot)
-            return inner
-
-        return lax.fori_loop(0, 4, one, carry)
-
-    lax.fori_loop(0, half - 1, ring_step, 0)
-
-    copy(0, n - 2, right).wait_recv()
-    copy(n - 2, n - 1, sibling).start()
-
-    def last_pair(k, carry):
-        @pl.when(k == 1)
+            copy(0, first, sibling).wait_recv()
+            copy(0, second, sibling).wait_recv()
+
+        @pl.when(p == last)
         def _():
-            copy(0, n - 1, sibling).wait_recv()
-
-        work(n - 2 + k)
-        return carry
-
-    lax.fori_loop(0, 2, last_pair, 0)
-
+            copy(0, first, right).wait_recv()
+            copy(first, second, sibling).start()
+            copy(0, second, sibling).wait_recv()
+
+        work(first, 2)
+        return carry
+
+    lax.fori_loop(0, last + 1, pair, 0)
+
+    for load in loads[3:]:
+        load.wait()
     d = direction[...]
     r = residual[...]
     image = (total[0:columns] + total[columns:]) * (outscale[0] * QUAD) + noise_var[0] * d
@@ -261,24 +268,29 @@
     )
     alpha = rr / curv
     rr_new = jnp.maximum(rr - 2.0 * alpha * ri + alpha * alpha * ii, 0.0)
-    fresh = r - alpha * image
-    new_solution[...] = solution[...] + alpha * d
-    new_residual[...] = fresh
-    new_direction[...] = fresh + (rr_new / rr) * d
+    image_out[...] = image
+    rates_out[...] = jnp.where(lane == 0, alpha, rr_new / rr)
 
 
 def shards(n, depth, features, inv_length, outscale, noise_var, solution, residual, direction):
     feats, points = features.shape
     columns = direction.shape[0]
+    hbm = pl.BlockSpec(memory_space=pltpu.HBM)
     vmem = pl.BlockSpec(memory_space=pltpu.VMEM)
-    smem = pl.BlockSpec(memory_space=pltpu.SMEM)
-    out = jax.ShapeDtypeStruct(direction.shape, jnp.float32)
-    return pl.pallas_call(
+    image, rates = pl.pallas_call(
         functools.partial(step_kernel, n, depth),
-        out_shape=(out, out, out),
-        in_specs=[vmem, smem, smem, smem, vmem, vmem, vmem],
-        out_specs=(vmem, vmem, vmem),
+        out_shape=(
+            jax.ShapeDtypeStruct(direction.shape, jnp.float32),
+            jax.ShapeDtypeStruct((columns, 128), jnp.float32),
+        ),
+        in_specs=[hbm] * 6,
+        out_specs=(vmem, vmem),
         scratch_shapes=[
+            pltpu.VMEM((feats, points), jnp.float32),
+            pltpu.SMEM((feats,), jnp.float32),
+            pltpu.SMEM((1,), jnp.float32),
+            pltpu.SMEM((1,), jnp.float32),
+            pltpu.VMEM((columns, points), jnp.float32),
             pltpu.VMEM((n, feats + columns, points), jnp.float32),
             pltpu.VMEM((8 * feats, points), jnp.bfloat16),
             pltpu.VMEM((2 * columns, points), jnp.float32),
@@ -288,11 +300,15 @@
             pltpu.SemaphoreType.DMA((n,)),
             pltpu.SemaphoreType.DMA((n,)),
             pltpu.SemaphoreType.DMA((n,)),
+            pltpu.SemaphoreType.DMA((6,)),
         ],
         compiler_params=pltpu.CompilerParams(
-            collective_id=0, has_side_effects=True, vmem_limit_bytes=24 * 1024 * 1024
+            collective_id=0, has_side_effects=True, vmem_limit_bytes=32 * 1024 * 1024
         ),
-    )(features, inv_length, outscale, noise_var, solution, residual, direction)
+    )(features, inv_length, outscale, noise_var, residual, direction)
+    alpha, beta = rates[:, 0:1], rates[:, 1:2]
+    new_residual = residual - alpha * image
+    return solution + alpha * direction, new_residual, new_residual + beta * direction
 
 
 def solution(mesh):

time: 34.8 us -> 30.7 us (0.88)
  local copies, waits for them, and re-layouts: 4.83 us -> 2.4 us
  Pallas kernels: 27.6 us -> 25.3 us
  other arithmetic: 0 us -> 0.72 us
    unnamed x13 -> x10, local copies, waits for them, and re-layouts: 4.83 us -> 2.23 us
    pallas_call x1, Pallas kernels: 27.6 us -> 25.3 us  [shards(): pl.pallas_call(functools.partial(step_kernel, n, depth), out_shape=(jax.S...]
    add x0 -> x1, other arithmetic: none -> 0.72 us  [shards(): new_residual + beta * direction]
where the time goes in v2:
time: 30.7 us; the launch traced here: 30.4 us
  Pallas kernels  25.3 us (82%)
  local copies, waits for them, and re-layouts  2.4 us (8%)
  between operations  1.98 us (6%)
  other arithmetic  0.72 us (2%)
    pallas_call x1, Pallas kernels, shards(): pl.pallas_call(functools.partial(step_kernel, n, depth), out_shape=(jax.S...  25.3 us
    unnamed x10, local copies, waits for them, and re-layouts  2.23 us
    add x1, other arithmetic, shards(): new_residual + beta * direction  0.72 us

profile of v2, /device:TPU:0, one launch (start us, length us, event | category | flops | bytes accessed | tf_op | source)
XLA Modules:
  0.0 30.4 jit_solution(4951936054349221802)
XLA Ops:
  1.3 0.0 copy-start.3
  1.9 0.0 copy-done.3
  2.0 0.0 copy-start
  2.0 0.7 %copy-done = f32[16,512]{1,0:T(8,128)S(1)} copy-done((f32[16,512]{1,0:T(8,128)S(1)}, f32[16,512]{1,0:T(8,128)}, u32[]{:S(2)}) %copy-start) | copy-done | bytes 32792
  2.7 0.0 copy-start.1
  2.7 0.8 %copy-done.1 = f32[16,512]{1,0:T(8,128)S(1)} copy-done((f32[16,512]{1,0:T(8,128)S(1)}, f32[16,512]{1,0:T(8,128)}, u32[]{:S(2)}) %copy-start.1) | copy-done | bytes 32792
  3.5 0.0 copy-start.2
  3.5 0.7 %copy-done.2 = f32[8,512]{1,0:T(8,128)S(1)} copy-done((f32[8,512]{1,0:T(8,128)S(1)}, f32[8,512]{1,0:T(8,128)}, u32[]{:S(2)}) %copy-start.2) | copy-done | bytes 16408
  4.2 0.0 copy-start.4
  4.2 25.3 %shard_map.94 = (f32[16,512]{1,0:T(8,128)S(1)}, f32[16,128]{1,0:T(8,128)S(1)}) custom-call(f32[8,512]{1,0:T(8,128)S(1)} %copy-done.2, f32[8]{0:T(128)S(1)} %copy-done.3, f32[1]{0:T(128)S(6)} %copy.10.outscale_hbm, f32[1]{0:T(128)S(6)} %copy.11.noise_var_hbm, f32[16,512]{1,0:T(8,128)S(1)} %copy-done.1, f32[16,512]{1,0:T(8,128)S(1)} %copy-done), custom_call_target="tpu_custom_call" | custom-call | tf_op jit(solution)/shard_map/pallas_call | solution.py:280
  29.5 0.2 slice_reduce_fusion
  29.6 0.0 copy-done.4
  29.7 0.7 %multiply_add_fusion = (f32[16,512]{1,0:T(8,128)}, f32[16,512]{1,0:T(8,128)}, f32[16,512]{1,0:T(8,128)}) fusion(f32[16,512]{1,0:T(8,128)S(1)} %copy-done, f32[16]{0:T(128)S(1)} %get-tuple-element.7, f32[16,512]{1,0:T(8,128)S(1)} %copy-done.1, f32[16,512]{1,0:T(8,128)S(1)} %get-tuple-element.6, f32[16]{0:T(128)S(1)} %get-tuple-element.8, f32[16,512]{1,0:T(8,128)S(1)} %copy-done.4), kind=kLoop, calls=%fused_computation | loop fusion | flops 49152 | bytes 229504 | tf_op jit(solution)/shard_map/add | solution.py:311
Async XLA Ops:
  1.3 0.7 %copy-start.3 = (f32[8]{0:T(128)S(1)}, f32[8]{0:T(128)}, u32[]{:S(2)}) copy-start(f32[8]{0:T(128)} %inv_length_hbm.1) | copy-start | bytes 100
  2.0 0.8 %copy-start = (f32[16,512]{1,0:T(8,128)S(1)}, f32[16,512]{1,0:T(8,128)}, u32[]{:S(2)}) copy-start(f32[16,512]{1,0:T(8,128)} %direction_hbm.1) | copy-start | bytes 98308
  2.7 0.8 %copy-start.1 = (f32[16,512]{1,0:T(8,128)S(1)}, f32[16,512]{1,0:T(8,128)}, u32[]{:S(2)}) copy-start(f32[16,512]{1,0:T(8,128)} %residual_hbm.1) | copy-start | bytes 98308
  3.5 0.7 %copy-start.2 = (f32[8,512]{1,0:T(8,128)S(1)}, f32[8,512]{1,0:T(8,128)}, u32[]{:S(2)}) copy-start(f32[8,512]{1,0:T(8,128)} %features_hbm.1) | copy-start | bytes 49156
  4.2 25.5 %copy-start.4 = (f32[16,512]{1,0:T(8,128)S(1)}, f32[16,512]{1,0:T(8,128)}, u32[]{:S(2)}) copy-start(f32[16,512]{1,0:T(8,128)} %param.11) | copy-start | bytes 98308

commit v3 on v2

--- a/solution.py
+++ b/solution.py
@@ -164,9 +164,8 @@
         tile = ((b + LIN) * b + CONST) * jnp.exp2(-b)
         high = tile.astype(jnp.bfloat16)
         low = (tile - high.astype(jnp.float32)).astype(jnp.bfloat16)
-        total[...] += jnp.dot(both, high, preferred_element_type=jnp.float32) + jnp.dot(
-            both, low, preferred_element_type=jnp.float32
-        )
+        total[...] += jnp.dot(both, high, preferred_element_type=jnp.float32)
+        total[0:columns] += jnp.dot(both[0:columns], low, preferred_element_type=jnp.float32)
 
     copy(0, 2, right).start()
     copy(0, 3, left).start()
@@ -303,7 +302,7 @@
             pltpu.SemaphoreType.DMA((6,)),
         ],
         compiler_params=pltpu.CompilerParams(
-            collective_id=0, has_side_effects=True, vmem_limit_bytes=32 * 1024 * 1024
+            collective_id=0, has_side_effects=True, vmem_limit_bytes=60 * 1024 * 1024
         ),
     )(features, inv_length, outscale, noise_var, residual, direction)
     alpha, beta = rates[:, 0:1], rates[:, 1:2]

time: 30.7 us -> 30.4 us (level)
  local copies, waits for them, and re-layouts: 2.4 us -> 0.97 us
  other arithmetic: 0.72 us -> 1.47 us
  Pallas kernels: 25.3 us -> 25.7 us
    unnamed x10 -> x6, local copies, waits for them, and re-layouts: 2.23 us -> 0.01 us
    slice x1, local copies, waits for them, and re-layouts: 0.17 us -> 0.95 us  [shards(): alpha, beta = (rates[:, 0:1], rates[:, 1:2])]
    add x1, other arithmetic: 0.72 us -> 1.47 us  [shards(): new_residual + beta * direction]
    pallas_call x1, Pallas kernels: 25.3 us -> 25.7 us  [shards(): pl.pallas_call(functools.partial(step_kernel, n, depth), out_shape=(jax.S...]
where the time goes in v3:
time: 30.4 us; the launch traced here: 30.1 us
  Pallas kernels  25.7 us (85%)
  between operations  1.97 us (6%)
  other arithmetic  1.47 us (5%)
  local copies, waits for them, and re-layouts  0.97 us (3%)
    pallas_call x1, Pallas kernels, shards(): pl.pallas_call(functools.partial(step_kernel, n, depth), out_shape=(jax.S...  25.7 us
    add x1, other arithmetic, shards(): new_residual + beta * direction  1.47 us
    slice x1, local copies, waits for them, and re-layouts, shards(): alpha, beta = (rates[:, 0:1], rates[:, 1:2])  0.95 us

profile of v3, /device:TPU:0, one launch (start us, length us, event | category | flops | bytes accessed | tf_op | source)
XLA Modules:
  0.0 30.1 jit_solution(348828530571411892)
XLA Ops:
  1.9 0.0 copy-start
  1.9 0.0 copy-start.1
  1.9 0.0 copy-start.2
  2.0 25.7 %shard_map.94 = (f32[16,512]{1,0:T(8,128)}, f32[16,128]{1,0:T(8,128)}) custom-call(f32[8,512]{1,0:T(8,128)} %features_hbm.1, f32[8]{0:T(128)} %inv_length_hbm.1, f32[1]{0:T(128)S(6)} %copy.10.outscale_hbm, f32[1]{0:T(128)S(6)} %copy.11.noise_var_hbm, f32[16,512]{1,0:T(8,128)} %residual_hbm.1, f32[16,512]{1,0:T(8,128)} %direction_hbm.1), custom_call_target="tpu_custom_call" | custom-call | tf_op jit(solution)/shard_map/pallas_call | solution.py:279
  27.7 1.0 %slice_reduce_fusion = (f32[16]{0:T(128)S(1)}, f32[16]{0:T(128)S(1)}) fusion(f32[16,128]{1,0:T(8,128)} %get-tuple-element.5), kind=kLoop, calls=%fused_computation.3 | loop fusion | bytes 256 | tf_op jit(solution)/shard_map/slice | solution.py:308
  28.6 0.0 copy-done
  28.6 0.0 copy-done.1
  28.6 0.0 copy-done.2
  28.7 1.5 %multiply_add_fusion = (f32[16,512]{1,0:T(8,128)}, f32[16,512]{1,0:T(8,128)}, f32[16,512]{1,0:T(8,128)}) fusion(f32[16,512]{1,0:T(8,128)S(1)} %copy-done, f32[16]{0:T(128)S(1)} %get-tuple-element.7, f32[16,512]{1,0:T(8,128)S(1)} %copy-done.1, f32[16,512]{1,0:T(8,128)} %get-tuple-element.6, f32[16]{0:T(128)S(1)} %get-tuple-element.8, f32[16,512]{1,0:T(8,128)S(1)} %copy-done.2), kind=kLoop, calls=%fused_computation | loop fusion | flops 49152 | bytes 229504 | tf_op jit(solution)/shard_map/add | solution.py:310
Async XLA Ops:
  1.9 26.7 %copy-start = (f32[16,512]{1,0:T(8,128)S(1)}, f32[16,512]{1,0:T(8,128)}, u32[]{:S(2)}) copy-start(f32[16,512]{1,0:T(8,128)} %direction_hbm.1) | copy-start | bytes 98308
  1.9 26.7 %copy-start.1 = (f32[16,512]{1,0:T(8,128)S(1)}, f32[16,512]{1,0:T(8,128)}, u32[]{:S(2)}) copy-start(f32[16,512]{1,0:T(8,128)} %residual_hbm.1) | copy-start | bytes 98308
  1.9 26.7 %copy-start.2 = (f32[16,512]{1,0:T(8,128)S(1)}, f32[16,512]{1,0:T(8,128)}, u32[]{:S(2)}) copy-start(f32[16,512]{1,0:T(8,128)} %param.11) | copy-start | bytes 98308
